TPU v7x, 512 devices: a whole 4x4x16 slice. The times are simulated.
512 devices in a mesh: tri: 64 (over y, z), sub: 8 (over x, core).
Axes of the slice: x: 4, y: 4, z: 16, core: 2. Of those that a mesh axis runs over, the one named last changes fastest.
Arguments:
- stored_tiles: float32 [64, 10, 512, 512], P('tri', None, 'sub'), may hold values from -190 to 190, as said below
- cell_owner: int32 [64], replicated, may hold values from 0 to 63, as said below
Outputs:
- updated: float32 [64, 10, 512, 512], P('tri', None, 'sub')
Inputs may be any that keep to these rules, and one draw needn't show every extreme that they name: `cell_owner`: a permutation of the indices of tri. `stored_tiles`: every tile whose row and column blocks are equal is skew-symmetric, every pivot met is invertible, and slots that hold no tile are zero.
All inputs are finite; a program needn't handle non-finite values.
Results may differ from a plain program's by a relative error of at most 0.00035.
Values may be sent and summed in bfloat16 or wider, within the bound.
A program may use at most 64 MiB of HBM per device.

v0:
```python
import math

import jax
import jax.numpy as jnp
import numpy as np
from jax import lax
from jax.sharding import Mesh
from jax.sharding import PartitionSpec as P

NB = 32
TRI = ("tri_0", "tri_1")


def in_order(tiles, dim):
    tiles = jnp.moveaxis(tiles, 0, dim)
    dims = tiles.shape
    return tiles.reshape(*dims[:dim], dims[dim] * dims[dim + 1], *dims[dim + 2 :])


def gather_in_order(x, axes, turns):
    tiles = x[None]
    for k in turns:
        tiles = lax.all_gather(tiles, axes[k], axis=0, tiled=True)
    block = [lax.axis_size(axes[k]) for k in reversed(turns)]
    tiles = tiles.reshape(*block, *x.shape)
    turned = sorted(range(len(turns)), key=lambda place: turns[len(turns) - 1 - place])
    return tiles.transpose(*turned, *range(len(turns), tiles.ndim)).reshape(-1, *x.shape)


def gather_axes(x, axes, turns, dim):
    return in_order(gather_in_order(x, axes, turns), dim)


def layout(groups, per_group):
    half_group = per_group // 2
    slot_count = per_group * (per_group + 1) // 2
    row_table = np.full((groups * groups, slot_count), -1, np.int32)
    col_table = np.full((groups * groups, slot_count), -1, np.int32)
    for first_group in range(groups):
        for second_group in range(groups):
            cell_index = first_group * groups + second_group
            for inner_row in range(per_group):
                if first_group == second_group:
                    for inner_column in range(inner_row + 1):
                        slot_index = inner_row * (inner_row + 1) // 2 + inner_column
                        row_table[cell_index, slot_index] = first_group * per_group + inner_row
                        col_table[cell_index, slot_index] = first_group * per_group + inner_column
                else:
                    for inner_column in range(half_group):
                        slot_index = inner_row * half_group + inner_column
                        if first_group > second_group:
                            row_table[cell_index, slot_index] = first_group * per_group + inner_row
                            col_table[cell_index, slot_index] = (
                                second_group * per_group + inner_column
                            )
                        else:
                            row_table[cell_index, slot_index] = second_group * per_group + inner_row
                            col_table[cell_index, slot_index] = (
                                first_group * per_group + half_group + inner_column
                            )
    return (row_table, col_table)


def shards(stored_tiles, cell_owner):
    tri_count = lax.axis_size(TRI)
    groups = math.isqrt(tri_count)
    per_group = NB // groups
    half_group = per_group // 2
    strip_rows = stored_tiles.shape[2]
    block_order = stored_tiles.shape[3]
    row_table, col_table = layout(groups, per_group)
    position = lax.axis_index(TRI)
    my_cell = jnp.sum(jnp.where(cell_owner == position, jnp.arange(tri_count, dtype=jnp.int32), 0))
    cell_down = my_cell // groups
    cell_across = my_cell % groups
    row_group = jnp.maximum(cell_down, cell_across)
    col_group = jnp.minimum(cell_down, cell_across)
    my_rows = jnp.asarray(row_table)[my_cell]
    my_cols = jnp.asarray(col_table)[my_cell]
    row_local = jnp.clip(my_rows - row_group * per_group, 0, per_group - 1)
    col_local = jnp.clip(my_cols - col_group * per_group, 0, per_group - 1)
    holders = cell_owner[jnp.arange(groups) * groups]
    highest = lax.Precision.HIGHEST
    current = stored_tiles[0]
    lower_slots = np.array([member * half_group for member in range(per_group)], np.int32)
    first_slots = np.array(
        [member * (member + 1) // 2 if member > 0 else 0 for member in range(per_group)], np.int32
    )
    keep_first = np.array([1.0 if member > 0 else 0.0 for member in range(per_group)], np.float32)
    from_lower = current[lower_slots]
    from_first = current[first_slots] * keep_first[:, None, None]
    holder_part = jnp.where(cell_down > 0, from_lower, from_first)
    holder_part = jnp.where(cell_across == 0, holder_part, 0.0).astype(jnp.bfloat16)
    pivot_slot = 0 // 2
    pivot_part = jnp.where(my_cell == 0, current[pivot_slot], 0.0)
    piece_size = holder_part.size // tri_count
    spread_panel = lax.all_to_all(
        holder_part.reshape(tri_count, piece_size), TRI, split_axis=0, concat_axis=0, tiled=True
    )
    spread_pivot = lax.all_to_all(
        pivot_part.astype(jnp.bfloat16), TRI, split_axis=0, concat_axis=0, tiled=True
    ).astype(pivot_part.dtype)
    picked_panel = spread_panel[holders][:, None, :]
    picked_pivot = spread_pivot[holders[0]][None, :]
    whole_panel = gather_axes(picked_panel, TRI, (0, 1), 1)
    whole_pivot = gather_axes(picked_pivot.astype(jnp.bfloat16), TRI, (0, 1), 0).astype(
        picked_pivot.dtype
    )
    panels = whole_panel.reshape(groups, per_group, strip_rows, block_order)
    own_strips = panels[row_group]
    other_strips = panels[col_group]
    pivot_block = lax.all_gather(
        whole_pivot.astype(jnp.bfloat16), "sub", axis=0, tiled=True
    ).astype(whole_pivot.dtype)
    partner = lax.all_gather(other_strips, "sub", axis=1, tiled=True)
    gram_matrix = jnp.dot(pivot_block.T, pivot_block, precision=highest)
    factor = jnp.linalg.cholesky(gram_matrix)
    inverse = jax.scipy.linalg.cho_solve((factor, True), pivot_block.T)
    scaled = jnp.einsum(
        "irk,kc->irc", own_strips.astype(jnp.float32), inverse, precision=highest
    ).astype(jnp.bfloat16)
    left_slots = scaled[row_local]
    right_slots = partner[col_local]
    update = jnp.einsum("qrk,qck->qrc", left_slots, right_slots, preferred_element_type=jnp.float32)
    live_slots = (my_rows > 0) & (my_cols > 0)
    current = current + jnp.where(live_slots[:, None, None], update, 0.0)
    return current[None]


def solution(mesh):
    torus = Mesh(mesh.devices.reshape(4, 16, mesh.shape["sub"]), ("tri_0", "tri_1", "sub"))
    return jax.shard_map(
        shards,
        mesh=torus,
        in_specs=(P(TRI, None, "sub", None), P()),
        out_specs=P(TRI, None, "sub", None),
        check_vma=False,
    )
```

profile of v0, /device:TPU:1, one launch (start us, length us, event | category | flops | bytes accessed | tf_op | source)
XLA Modules:
  0.0 323.5 jit_solution(5538113034983923474)
XLA Ops:
  11.3 19.3 %all-to-all-start.1 = ((bf16[64,2,256]{2,1,0:T(2,128)(2,1)}), bf16[64,2,256]{2,1,0:T(2,128)(2,1)S(1)}, u32[]{:S(2)}, u32[]{:S(2)}) async-start(bf16[64,2,256]{2,1,0:T(2,128)(2,1)} %reshape.305), calls=%async_computation.1 | async-start | bytes 131072 | tf_op jit(solution)/shard_map/all_to_all | solution.py:100
  43.2 2.1 reduce.26
  46.2 14.6 %all-to-all-start = ((bf16[64,2,1024]{2,1,0:T(2,128)(2,1)}), bf16[64,2,1024]{2,1,0:T(2,128)(2,1)S(1)}, u32[]{:S(2)}, u32[]{:S(2)}) async-start(bf16[64,2,1024]{2,1,0:T(2,128)(2,1)} %reshape.307), calls=%async_computation | async-start | bytes 524288 | tf_op jit(solution)/shard_map/all_to_all | solution.py:97
  60.9 8.8 %all_gather.20 = bf16[4,1,512]{2,1,0:T(2,128)(2,1)S(1)} all-gather(bf16[1,1,512]{2,1,0:T(2,128)(2,1)S(1)} %fusion.54), channel_id=1, replica_groups=mesh['tri_0'=4,'tri_1'=16,'sub'=8] {'tri_0'}, dimensions={0}, use_global_device_ids=true | all-gather | bytes 5120 | tf_op jit(solution)/shard_map/all_gather | solution.py:23
  69.7 23.8 %all_gather.21 = bf16[64,1,512]{2,1,0:T(2,128)(2,1)S(1)} all-gather(bf16[4,1,512]{2,1,0:T(2,128)(2,1)S(1)} %all_gather.20), channel_id=1, replica_groups=mesh['tri_0'=4,'tri_1'=16,'sub'=8] {'tri_1'}, dimensions={0}, use_global_device_ids=true | all-gather | bytes 69632 | tf_op jit(solution)/shard_map/all_gather | solution.py:23
  93.9 23.6 %all_gather.22 = bf16[512,512]{1,0:T(8,128)(2,1)S(1)} all-gather(bf16[64,512]{1,0:T(8,128)(2,1)S(1)} %bitcast.120), channel_id=1, replica_groups=mesh['tri_0'=4,'tri_1'=16,'sub'=8] {'sub'}, dimensions={0}, use_global_device_ids=true | all-gather | bytes 589824 | tf_op jit(solution)/shard_map/all_gather | solution.py:112
  119.6 11.7 %cholesky.104 = f32[128,128]{1,0:T(8,128)S(1)} custom-call(f32[128,128]{1,0:T(8,128)S(1)} %cholesky.266), custom_call_target="Cholesky" | custom-call | tf_op jit(solution)/shard_map/jit(cholesky)/cholesky | solution.py:117
  131.3 9.8 %custom-call.34 = f32[1,128,128]{1,2,0:T(8,128)S(1)} custom-call(f32[1,128,128]{2,1,0:T(8,128)S(1)} %get-tuple-element.32), custom_call_target="InvertDiagBlocksLowerTriangular" | custom-call | tf_op jit(solution)/shard_map/jit(cholesky)/cholesky | solution.py:117
  142.3 9.8 %all-gather = bf16[32,2048]{1,0:T(8,128)(2,1)} all-gather(bf16[8,2048]{1,0:T(8,128)(2,1)S(1)} %gather_fusion.3), channel_id=2, replica_groups=mesh['tri_0'=4,'tri_1'=16,'sub'=8] {'tri_0'}, dimensions={0}, use_global_device_ids=true | all-gather | bytes 163840 | tf_op jit(solution)/shard_map/all_gather | solution.py:23
  154.3 11.7 %cholesky.217 = f32[128,128]{1,0:T(8,128)S(1)} custom-call(f32[128,128]{1,0:T(8,128)S(1)} %cholesky.270), custom_call_target="Cholesky" | custom-call | tf_op jit(solution)/shard_map/jit(cholesky)/cholesky | solution.py:117
  166.0 9.8 %custom-call.35 = f32[1,128,128]{1,2,0:T(8,128)S(1)} custom-call(f32[1,128,128]{2,1,0:T(8,128)S(1)} %get-tuple-element.29), custom_call_target="InvertDiagBlocksLowerTriangular" | custom-call | tf_op jit(solution)/shard_map/jit(cholesky)/cholesky | solution.py:117
  176.5 11.7 %cholesky.238 = f32[128,128]{1,0:T(8,128)S(1)} custom-call(f32[128,128]{1,0:T(8,128)S(1)} %cholesky.275), custom_call_target="Cholesky" | custom-call | tf_op jit(solution)/shard_map/jit(cholesky)/cholesky | solution.py:117
  188.3 9.9 %custom-call.36 = f32[1,128,128]{1,2,0:T(8,128)S(1)} custom-call(f32[1,128,128]{2,1,0:T(8,128)S(1)} %get-tuple-element.26), custom_call_target="InvertDiagBlocksLowerTriangular" | custom-call | tf_op jit(solution)/shard_map/jit(cholesky)/cholesky | solution.py:117
  198.8 11.7 %cholesky.255 = f32[128,128]{1,0:T(8,128)S(1)} custom-call(f32[128,128]{1,0:T(8,128)S(1)} %convolution_subtract_fusion.8), custom_call_target="Cholesky" | custom-call | tf_op jit(solution)/shard_map/jit(cholesky)/cholesky | solution.py:117
  215.6 10.8 %while.1 = (s32[]{:T(128)}, f32[512,512]{1,0:T(8,128)S(1)}, s32[4,2]{0,1:T(2,128)S(1)}, f32[4,128,128]{2,1,0:T(8,128)}, s32[]{:T(128)}) while((s32[]{:T(128)}, f32[512,512]{1,0:T(8,128)S(1)}, s32[4,2]{0,1:T(2,128)S(1)}, f32[4,128,128]{2,1,0:T(8,128)}, s32[]{:T(128)}) %tuple.27), condition=%wide.while_cond, body=%wide.while_body.sunk | while | flops 2 | bytes 132705 | solution.py:118
  216.3 2.0 bitcast_dynamic-update-slice_fusion.2
  219.0 2.0 bitcast_dynamic-update-slice_fusion.2
  221.7 2.0 bitcast_dynamic-update-slice_fusion.2
  224.4 2.0 bitcast_dynamic-update-slice_fusion.2
  226.4 40.1 %custom-call.37 = f32[4,128,128]{1,2,0:T(8,128)S(1)} custom-call(f32[4,128,128]{2,1,0:T(8,128)} %get-tuple-element.12), custom_call_target="InvertDiagBlocksLowerTriangular" | custom-call | tf_op jit(solution)/shard_map/jit(_cho_solve)/triangular_solve | solution.py:118
  269.5 2.6 reshape_reshape.6
  284.2 21.5 %all-gather.7.cloned.1.call-done = bf16[1,4,512,512]{3,2,1,0:T(8,128)(2,1)} async-done(((bf16[1,4,64,512]{3,2,1,0:T(8,128)(2,1)}), bf16[1,4,512,512]{3,2,1,0:T(8,128)(2,1)}) %all-gather.7.cloned.1.call-update) | async-done | bytes 2097168 | tf_op jit(solution)/shard_map/all_gather | solution.py:115
  305.8 5.4 %gather_fusion.5 = bf16[10,512,512]{2,1,0:T(8,128)(2,1)} fusion(bf16[4,512,512]{2,1,0:T(8,128)(2,1)} %bitcast.112, s32[1024]{0:T(1024)S(1)} %pad_clamp_fusion), kind=kCustom, calls=%fused_computation.5 | custom fusion | bytes 10485800 | tf_op jit(solution)/shard_map/gather | solution.py:123
  311.2 5.2 %fusion.1 = f32[1,10,64,512]{3,2,1,0:T(8,128)} fusion(bf16[10,64,512]{2,1,0:T(8,128)(2,1)S(1)} %gather_fusion.4, bf16[10,512,512]{2,1,0:T(8,128)(2,1)} %gather_fusion.5, pred[10]{0:T(512)(128)(4,1)S(1)} %and_bitcast_fusion, f32[1,10,64,512]{3,2,1,0:T(8,128)S(1)} %copy-done), kind=kOutput, calls=%fused_computation.10 | convolution fusion | flops 336199680 | bytes 8519690 | tf_op jit(solution)/shard_map/qrk,qck->qrc/dot_general | solution.py:124
  (99 shorter events, 40.2 us)
Async XLA Ops:
  6.5 35.5 %copy-start.3 = (f32[4]{0:T(128)S(1)}, f32[4]{0:T(128)}, u32[]{:S(2)}) copy-start(f32[4]{0:T(128)} %constant.245) | copy-start | bytes 52
  11.3 34.9 %all-to-all-start.1 = ((bf16[64,2,256]{2,1,0:T(2,128)(2,1)}), bf16[64,2,256]{2,1,0:T(2,128)(2,1)S(1)}, u32[]{:S(2)}, u32[]{:S(2)}) async-start(bf16[64,2,256]{2,1,0:T(2,128)(2,1)} %reshape.305), calls=%async_computation.1 | async-start | bytes 131072 | tf_op jit(solution)/shard_map/all_to_all | solution.py:100
  46.2 95.1 %all-to-all-start = ((bf16[64,2,1024]{2,1,0:T(2,128)(2,1)}), bf16[64,2,1024]{2,1,0:T(2,128)(2,1)S(1)}, u32[]{:S(2)}, u32[]{:S(2)}) async-start(bf16[64,2,1024]{2,1,0:T(2,128)(2,1)} %reshape.307), calls=%async_computation | async-start | bytes 524288 | tf_op jit(solution)/shard_map/all_to_all | solution.py:97
  60.8 205.8 %all-gather.5.cloned.1.call-start = ((), (), s32[]{:S(2)}) async-start(), calls=%async_computation.2 | async-start | bytes 2228224 | tf_op jit(solution)/shard_map/all_gather | solution.py:23
  118.6 1.0 copy-start.1
  119.6 33.0 %copy-start.2 = (f32[512,512]{1,0:T(8,128)S(1)}, f32[512,512]{1,0:T(8,128)}, u32[]{:S(2)}) copy-start(f32[512,512]{1,0:T(8,128)} %copy-done.1) | copy-start | bytes 3145732
  152.1 153.6 %all-gather.7.cloned.1.call-start = ((), (), s32[]{:S(2)}) async-start(), calls=%async_computation.3 | async-start | bytes 2359296 | tf_op jit(solution)/shard_map/all_gather | solution.py:115
  305.8 5.4 %copy-start = (f32[1,10,64,512]{3,2,1,0:T(8,128)S(1)}, f32[1,10,64,512]{3,2,1,0:T(8,128)}, u32[]{:S(2)}) copy-start(f32[1,10,64,512]{3,2,1,0:T(8,128)} %param.9) | copy-start | bytes 3932164
Sparse Core Ops, SparseCore 0:
  152.3 63.3 all-gather.4
  273.9 31.7 all-gather.6
where the time goes:
time: 329 us; the launch traced here: 323 us
  other arithmetic  129 us (39%)
  blocking collectives  66.1 us (20%)
  local copies, waits for them, and re-layouts  34.8 us (11%)
  starting transfers between devices  34.3 us (10%)
  between operations  21.8 us (7%)
  waiting for transfers between devices  21.6 us (7%)
  matrix products  16.1 us (5%)
    another operation x14, other arithmetic, shards(): factor = jnp.linalg.cholesky(gram_matrix)  78.7 us
    all_gather x3, blocking collectives, gather_in_order(): tiles = lax.all_gather(tiles, axes[k], axis=0, tiled=True)  42.5 us
    another operation x3, other arithmetic, shards(): inverse = jax.scipy.linalg.cho_solve((factor, True), pivot_block.T)  40.3 us
    all_gather x1, blocking collectives, shards(): lax.all_gather(whole_pivot.astype(jnp.bfloat16), 'sub', axis=0, tiled=True)  23.6 us
    all_gather x1, waiting for transfers between devices, shards(): partner = lax.all_gather(other_strips, 'sub', axis=1, tiled=True)  21.5 us
    all_to_all x1, starting transfers between devices, shards(): lax.all_to_all(pivot_part.astype(jnp.bfloat16), TRI, split_axis=0, concat...  19.3 us
    all_to_all x1, starting transfers between devices, shards(): lax.all_to_all(holder_part.reshape(tri_count, piece_size), TRI, split_axi...  14.6 us
    another operation x12, local copies, waits for them, and re-layouts  10.8 us
  transfers between devices with their start and end apart: 4, of which 1 were waited for; matrix products, arithmetic and copies ran while one was open for 48% of the time, Pallas kernels for 0%

commit v1 on v0

v1 whole, which is shorter than its diff:
```python
import functools

import jax
import jax.numpy as jnp
from jax import lax
from jax.experimental import pallas as pl
from jax.experimental.pallas import tpu as pltpu
from jax.sharding import Mesh
from jax.sharding import PartitionSpec as P

MESH = pl.DeviceIdType.MESH
AXES = ("y", "z", "x", "c")
NY, NZ, NX, NC = 4, 16, 4, 2
TRI = NY * NZ
SUB = NX * NC
GROUPS = 8
PER = 4
N = 512
ROWS = N // SUB
LANES = 128
CB = N // LANES
PIECE = 16
LOAD_SLOTS = (0, 1, 2, 3, 4, 6)
FIRST_SLOTS = (0, 1, 3, 6)
NEWTON_STEPS = 6
NEWTON_LOW = 0.004
BF = jnp.bfloat16
F32 = jnp.float32


def drain(ref, sem):
    pltpu.make_async_copy(ref, ref, sem).wait()


def send(src, dst, send_sem, recv_sem, device):
    pltpu.make_async_remote_copy(
        src_ref=src,
        dst_ref=dst,
        send_sem=send_sem,
        recv_sem=recv_sem,
        device_id=device,
        device_id_type=MESH,
    ).start()


def cells_at(owner_ref, places):
    def body(c, found):
        owner = owner_ref[c]
        return tuple(jnp.where(owner == t, c, f) for t, f in zip(places, found))

    zero = jnp.int32(0)
    return lax.fori_loop(0, TRI, body, tuple(zero for _ in places))


def groups_of(cell):
    down = lax.shift_right_logical(cell, jnp.int32(3))
    across = lax.bitwise_and(cell, jnp.int32(7))
    first = jnp.where(down < across, 2, 0)
    return jnp.maximum(down, across), jnp.minimum(down, across), first


def route_kernel(
    owner_ref,
    tiles_ref,
    fin,
    right,
    piv,
    loaded,
    panel,
    a2r,
    yb,
    msg,
    pyr,
    psel,
    wz,
    mz,
    load_sem,
    p_send,
    p_recv,
    a_send,
    a_recv,
    m_send,
    m_recv,
    y_send,
    y_recv,
    w_send,
    w_recv,
    x_send,
    x_recv,
    c_send,
    c_recv,
    q_send,
    q_recv,
):
    y, z = lax.axis_index("y"), lax.axis_index("z")
    x, c = lax.axis_index("x"), lax.axis_index("c")
    me = y * NZ + z
    u = x * NC + c
    res = lax.rem(z, 4)
    quo = z // 4
    far2 = 2 + 12 * c
    window = (1, 15, far2)
    mates = (4, 12, 8)
    others4 = (1, 3, 2)

    for k, slot in enumerate(LOAD_SLOTS):
        pltpu.make_async_copy(tiles_ref.at[0, slot], loaded.at[k], load_sem).start()

    barrier = pltpu.get_barrier_semaphore()

    def greet(k, carry):
        ty, tz = lax.rem(y + k // NZ, NY), lax.rem(z + lax.rem(k, NZ), NZ)
        pl.semaphore_signal(barrier, inc=1, device_id=(ty, tz, x, c), device_id_type=MESH)
        return carry

    lax.fori_loop(1, TRI, greet, 0)
    for dx in others4:
        pl.semaphore_signal(
            barrier, inc=1, device_id=(y, z, lax.rem(x + dx, NX), c), device_id_type=MESH
        )
    pl.semaphore_signal(barrier, inc=1, device_id=(y, z, x, 1 - c), device_id_type=MESH)

    tri_of = lambda dz: y * NZ + lax.rem(z + dz, NZ)
    cells = cells_at(owner_ref, (me, tri_of(1), tri_of(15), tri_of(far2)))
    pivot_at = owner_ref[0]
    y0 = lax.shift_right_logical(pivot_at, jnp.int32(4))
    z0 = lax.bitwise_and(pivot_at, jnp.int32(15))

    drain(loaded, load_sem)
    is_first = cells[0] < GROUPS
    for i in range(PER):
        low = loaded[LOAD_SLOTS.index(2 * i)]
        top = loaded[LOAD_SLOTS.index(FIRST_SLOTS[i])]
        tile = jnp.where(is_first, top, low).astype(BF)
        for b in range(CB):
            panel[i, b] = tile[:, b * LANES : (b + 1) * LANES]
    pl.semaphore_wait(barrier, TRI - 1 + 4)

    def spread(lo, hi):
        def body(k, carry):
            ty, tz = lax.rem(y + k // NZ, NY), lax.rem(z + lax.rem(k, NZ), NZ)
            row = pl.multiple_of((tz // 4) * PIECE, PIECE)
            send(
                panel.at[ty, lax.rem(tz, 4), pl.ds(row, PIECE)],
                a2r.at[me],
                a_send,
                a_recv,
                (ty, tz, x, c),
            )
            return carry

        lax.fori_loop(lo, hi, body, 0)

    my_row = pl.multiple_of(quo * PIECE, PIECE)
    res_row = pl.multiple_of(res * PIECE, PIECE)

    for k, dy in enumerate(others4):
        ty = lax.rem(y + dy, NY)
        send(panel.at[0, ty], pyr.at[y], p_send.at[0], p_recv.at[0], (ty, z, x, c))
    pyr[y] = panel[0, y]
    spread(1, 16)
    drain(pyr.at[0:3], p_recv.at[0])
    psel[...] = pyr[y0]
    for k, dz in enumerate(window):
        tz = lax.rem(z + dz, NZ)
        row = pl.multiple_of(lax.rem(tz, 4) * PIECE, PIECE)
        send(
            psel.at[pl.ds(row, PIECE)], wz.at[k + 1], p_send.at[1], p_recv.at[1], (y, tz, x, c)
        )
    wz[0] = psel[pl.ds(res_row, PIECE)]
    spread(16, 32)
    drain(wz.at[0:3], p_recv.at[1])
    delta = lax.bitwise_and(z - z0, 15)
    came = jnp.where(delta == 1, 1, jnp.where(delta == 15, 2, jnp.where(delta == far2, 3, 0)))
    mz[0] = wz[came]
    for k, dz in enumerate(mates):
        send(
            mz.at[0],
            mz.at[k + 1],
            p_send.at[2],
            p_recv.at[2],
            (y, lax.rem(z + dz, NZ), x, c),
        )
    spread(32, 48)
    drain(mz.at[1:4], p_recv.at[2])
    came = jnp.int32(0)
    for k, dz in enumerate(mates):
        delta = lax.bitwise_and(z - dz - z0, 15)
        valid = (delta == 0) | (delta == 1) | (delta == 15) | (delta == far2)
        came = jnp.where(valid, k + 1, came)
    part = piv.at[u, y]
    part[pl.ds(res_row, PIECE)] = mz[came]
    for k, dz in enumerate(window):
        send(
            part.at[pl.ds(res_row, PIECE)],
            part.at[pl.ds(res_row, PIECE)],
            p_send.at[3],
            p_recv.at[3],
            (y, lax.rem(z + dz, NZ), x, c),
        )
    spread(48, 64)
    drain(mz.at[1:4], p_recv.at[3])
    for k, dy in enumerate(others4):
        send(part, part, p_send.at[4], p_recv.at[4], (lax.rem(y + dy, NY), z, x, c))
    drain(pyr.at[0:3], p_recv.at[4])
    strip = piv.at[u]
    for k, dx in enumerate(others4):
        send(strip, strip, p_send.at[5], q_recv.at[k], (y, z, lax.rem(x + dx, NX), c))
    send(strip, strip, q_send, p_recv.at[5], (y, z, x, 1 - c))

    a2r[me] = panel[y, res, pl.ds(my_row, PIECE)]
    drain(a2r.at[0 : TRI - 1], a_recv)
    gathered = yb.at[y]
    for g in range(GROUPS):
        gathered[g, pl.ds(my_row, PIECE)] = a2r[owner_ref[g * GROUPS]]
    for k, dz in enumerate(mates):
        piece = gathered.at[:, pl.ds(my_row, PIECE)]
        send(piece, piece, m_send, m_recv, (y, lax.rem(z + dz, NZ), x, c))

    for k, dx in enumerate(others4):
        drain(strip, q_recv.at[k])
        source = lax.rem(x - dx + NX, NX) * NC + c
        send(piv.at[source], piv.at[source], q_send, p_recv.at[5], (y, z, x, 1 - c))

    drain(gathered.at[:, 0 : 3 * PIECE], m_recv)
    for k, dy in enumerate(others4):
        send(gathered, gathered, y_send, y_recv, (lax.rem(y + dy, NY), z, x, c))
    drain(yb.at[0:3], y_recv)

    def pick(cell, out):
        row_group, col_group, first = groups_of(cell)
        for i in range(PER):
            out[i] = yb[i, row_group]
        for j in range(2):
            out[PER + j] = yb[first + j, col_group]

    for k, dz in enumerate(window):
        pick(cells[k + 1], msg.at[k])
        send(
            msg.at[k], fin.at[res], w_send, w_recv.at[k], (y, lax.rem(z + dz, NZ), x, c)
        )
    pick(cells[0], fin.at[res])

    for part_no in range(4):
        if part_no > 0:
            drain(msg.at[0], w_recv.at[part_no - 1])
        b = lax.rem(z - (0, 1, 15, far2)[part_no] + NZ, 4)
        right[u, b] = fin[b, 2:6]
        for k, dx in enumerate(others4):
            send(
                fin.at[b, 2:6],
                right.at[u, b],
                x_send,
                x_recv.at[part_no, k],
                (y, z, lax.rem(x + dx, NX), c),
            )
        send(fin.at[b, 2:6], right.at[u, b], c_send, c_recv, (y, z, x, 1 - c))
    for part_no in range(4):
        b = lax.rem(z - (0, 1, 15, far2)[part_no] + NZ, 4)
        for k, dx in enumerate(others4):
            drain(right.at[0, 0], x_recv.at[part_no, k])
            source = lax.rem(x - dx + NX, NX) * NC + c
            send(right.at[source, b], right.at[source, b], c_send, c_recv, (y, z, x, 1 - c))
    drain(right.at[0:4], c_recv)
    drain(piv.at[0:4], p_recv.at[5])

    drain(pyr.at[0:3], p_send.at[0])
    drain(wz.at[0:3], p_send.at[1])
    drain(mz.at[1:4], p_send.at[2])
    drain(mz.at[1:4], p_send.at[3])
    drain(pyr.at[0:3], p_send.at[4])
    drain(piv.at[0:3], p_send.at[5])
    drain(piv.at[0:4], q_send)
    drain(a2r.at[0 : TRI - 1], a_send)
    drain(gathered.at[:, 0 : 3 * PIECE], m_send)
    drain(yb.at[0:3], y_send)
    drain(msg, w_send)
    drain(right.at[0:3], x_send)
    drain(right.at[0:4], c_send)


def dot(a, b, precision=None):
    return lax.dot_general(
        a, b, (((1,), (0,)), ((), ())), precision=precision, preferred_element_type=F32
    )


def dot_nt(a, b):
    return lax.dot_general(a, b, (((1,), (1,)), ((), ())), preferred_element_type=F32)


def schedule(low, steps):
    out, scale = [], 1.0
    for _ in range(steps):
        s = (1 + low) / (1 - low)
        t = 2 * s * s - 1
        out.append((8 * (1 + low) / (1 - low) ** 2 / t / scale, 8 / (1 - low) ** 2 / t / scale**2))
        scale, low = 1 + 1 / t, (1 - 1 / t) / (1 + 1 / t)
    return out


def identity():
    shape = (N, N)
    return lax.broadcasted_iota(jnp.int32, shape, 0) == lax.broadcasted_iota(jnp.int32, shape, 1)


def newton(p, xb, yv):
    yv[...] = dot_nt(p[...], p[...])
    bound = jnp.max(jnp.sum(jnp.abs(yv[...]), axis=0, keepdims=True))
    inv = 1.0 / bound
    xb[...] = (p[...].astype(F32) * -inv).astype(BF)
    yv[...] = yv[...] * inv
    coefs = schedule(NEWTON_LOW, NEWTON_STEPS)

    def step(k, carry):
        c1, c2 = jnp.float32(coefs[0][0]), jnp.float32(coefs[0][1])
        for i in range(1, NEWTON_STEPS):
            c1 = jnp.where(k == i, coefs[i][0], c1)
            c2 = jnp.where(k == i, coefs[i][1], c2)
        m = (jnp.where(identity(), c1, 0.0) - c2 * yv[...]).astype(BF)
        xb[...] = dot(xb[...], m).astype(BF)
        yv[...] = dot(p[...], xb[...])
        return carry

    lax.fori_loop(0, NEWTON_STEPS, step, 0)


def update_kernel(
    owner_ref, tiles_ref, fin, right, piv, out_ref, cur, p, xb, xf, yv, rt, left, in_sem, out_sem
):
    for slot in range(10):
        pltpu.make_async_copy(tiles_ref.at[0, slot], cur.at[slot], in_sem.at[slot]).start()
    me = lax.axis_index("y") * NZ + lax.axis_index("z")
    (cell,) = cells_at(owner_ref, (me,))
    row_group, col_group, first = groups_of(cell)
    diagonal = row_group == col_group

    for v in range(SUB):
        for b in range(CB):
            p[v * ROWS : (v + 1) * ROWS, b * LANES : (b + 1) * LANES] = piv[v, b]
    newton(p, xb, yv)

    yv[...] = jnp.where(identity(), 1.0, 0.0) - yv[...]
    xf[...] = xb[...].astype(F32)
    highest = lax.Precision.HIGHEST
    size = jnp.sum(yv[...] * yv[...])

    @pl.when(jnp.logical_not(size < 0.01))
    def _():
        @pl.when(jnp.logical_not(size < 0.25))
        def _():
            whole = p[...].astype(F32)
            rows = jnp.max(jnp.sum(jnp.abs(whole), axis=0, keepdims=True))
            xf[...] = whole * (-1.0 / rows) / rows

        def residual():
            yv[...] = jnp.where(identity(), 1.0, 0.0) - dot(
                p[...].astype(F32), xf[...], highest
            )
            return jnp.sum(yv[...] * yv[...])

        def more(carry):
            k, size = carry
            xf[...] = xf[...] + dot(xf[...], yv[...], highest)
            return k + 1, residual()

        lax.while_loop(lambda s: (s[0] < 150) & (s[1] > 0.001), more, (0, residual()))

    small = yv[...].astype(BF)
    yv[...] = yv[...] + dot(small, small)
    xf[...] = xf[...] + dot(xf[...].astype(BF), yv[...].astype(BF))

    high = xf[...].astype(BF)
    xb[...] = high
    xf[...] = xf[...] - high.astype(F32)
    for i in range(PER):
        strip = jnp.concatenate([fin[b, i] for b in range(CB)], axis=1)
        left[i * ROWS : (i + 1) * ROWS] = (
            dot(strip, xb[...]) + dot(strip, xf[...].astype(BF))
        ).astype(BF)

    def stage(j, strip):
        for v in range(SUB):
            for b in range(CB):
                rt[j, v * ROWS : (v + 1) * ROWS, b * LANES : (b + 1) * LANES] = right[v, b, strip]

    for slot in range(10):
        pltpu.make_async_copy(tiles_ref.at[0, slot], cur.at[slot], in_sem.at[slot]).wait()
    stage(0, 2)
    stage(1, 3)

    @pl.when(diagonal)
    def _():
        stage(2, 0)
        stage(3, 1)
        for j in range(PER):
            live = (row_group > 0) | (j > 0)
            product = dot_nt(left[j * ROWS :], rt[j])
            for i in range(j, PER):
                slot = i * (i + 1) // 2 + j
                term = product[(i - j) * ROWS : (i - j + 1) * ROWS]
                cur[slot] = cur[slot] + jnp.where(live, term, 0.0)

    @pl.when(jnp.logical_not(diagonal))
    def _():
        for j in range(2):
            live = col_group * PER + first + j > 0
            product = dot_nt(left[...], rt[j])
            for i in range(PER):
                slot = 2 * i + j
                term = product[i * ROWS : (i + 1) * ROWS]
                cur[slot] = cur[slot] + jnp.where(live, term, 0.0)

    for slot in range(10):
        pltpu.make_async_copy(cur.at[slot], out_ref.at[0, slot], out_sem.at[slot]).start()
    for slot in range(10):
        pltpu.make_async_copy(cur.at[slot], out_ref.at[0, slot], out_sem.at[slot]).wait()


def shards(stored_tiles, cell_owner):
    dma = pltpu.SemaphoreType.DMA
    vmem = pl.BlockSpec(memory_space=pltpu.VMEM)
    smem = pl.BlockSpec(memory_space=pltpu.SMEM)
    hbm = pl.BlockSpec(memory_space=pl.ANY)
    strip = (ROWS, LANES)
    fin, right, piv = pl.pallas_call(
        route_kernel,
        out_shape=(
            jax.ShapeDtypeStruct((CB, 6, *strip), BF),
            jax.ShapeDtypeStruct((SUB, CB, 4, *strip), BF),
            jax.ShapeDtypeStruct((SUB, CB, *strip), BF),
        ),
        in_specs=[smem, hbm],
        out_specs=(vmem, vmem, vmem),
        scratch_shapes=[
            pltpu.VMEM((len(LOAD_SLOTS), ROWS, N), F32),
            pltpu.VMEM((PER, CB, *strip), BF),
            pltpu.VMEM((TRI, PIECE, LANES), BF),
            pltpu.VMEM((PER, GROUPS, *strip), BF),
            pltpu.VMEM((3, 6, *strip), BF),
            pltpu.VMEM((NY, *strip), BF),
            pltpu.VMEM(strip, BF),
            pltpu.VMEM((4, PIECE, LANES), BF),
            pltpu.VMEM((4, PIECE, LANES), BF),
            dma,
            dma((6,)),
            dma((6,)),
            dma,
            dma,
            dma,
            dma,
            dma,
            dma,
            dma,
            dma((3,)),
            dma,
            dma((4, 3)),
            dma,
            dma,
            dma,
            dma((3,)),
        ],
        compiler_params=pltpu.CompilerParams(
            collective_id=0, has_side_effects=True, vmem_limit_bytes=40 * 2**20
        ),
    )(cell_owner, stored_tiles)
    return pl.pallas_call(
        update_kernel,
        out_shape=jax.ShapeDtypeStruct(stored_tiles.shape, F32),
        in_specs=[smem, hbm, vmem, vmem, vmem],
        out_specs=hbm,
        scratch_shapes=[
            pltpu.VMEM((10, ROWS, N), F32),
            pltpu.VMEM((N, N), BF),
            pltpu.VMEM((N, N), BF),
            pltpu.VMEM((N, N), F32),
            pltpu.VMEM((N, N), F32),
            pltpu.VMEM((PER, N, N), BF),
            pltpu.VMEM((PER * ROWS, N), BF),
            dma((10,)),
            dma((10,)),
        ],
        compiler_params=pltpu.CompilerParams(vmem_limit_bytes=40 * 2**20),
    )(cell_owner, stored_tiles, fin, right, piv)


def solution(mesh):
    torus = Mesh(mesh.devices.reshape(NY, NZ, NX, NC), AXES)
    spec = P(("y", "z"), None, ("x", "c"), None)
    return jax.shard_map(
        shards, mesh=torus, in_specs=(spec, P()), out_specs=spec, check_vma=False
    )
```

time: 329 us -> 86.7 us (0.26); the launches traced: 323 us -> 85.7 us
  other arithmetic: 129 us -> 0 us
  Pallas kernels: 0 us -> 83.7 us
  blocking collectives: 66.1 us -> 0 us
  starting transfers between devices: 34.3 us -> 0 us
  local copies, waits for them, and re-layouts: 34.8 us -> 1.97 us
  between operations: 21.8 us -> 0.01 us
  waiting for transfers between devices: 21.6 us -> 0 us
  matrix products: 16.1 us -> 0 us
    another operation x18 -> x0, other arithmetic: 119 us -> none  [the longest x14 78.7 us: shards(): factor = jnp.linalg.cholesky(gram_matrix)]
    pallas_call x0 -> x2, Pallas kernels: none -> 83.7 us  [the longest x1 71 us: shards(): pl.pallas_call(route_kernel, out_shape=(jax.ShapeDtypeStruct((CB, 6, *str...]
    all_gather x4 -> x0, blocking collectives: 66.1 us -> none  [the longest x3 42.5 us: gather_in_order(): tiles = lax.all_gather(tiles, axes[k], axis=0, tiled=True)]
    all_to_all x2 -> x0, starting transfers between devices: 33.9 us -> none  [the longest x1 19.3 us: shards(): lax.all_to_all(pivot_part.astype(jnp.bfloat16), TRI, split_axis=0, concat...]
    all_gather x2 -> x0, waiting for transfers between devices: 21.5 us -> none  [the longest x1 21.5 us: shards(): partner = lax.all_gather(other_strips, 'sub', axis=1, tiled=True)]
    another operation x18 -> x0, local copies, waits for them, and re-layouts: 13.6 us -> none
    gather x6 -> x0, local copies, waits for them, and re-layouts: 11.7 us -> none  [the longest x1 5.44 us: shards(): right_slots = partner[col_local]]
    another operation x20 -> x0, matrix products: 8.78 us -> none  [the longest x14 6.91 us: shards(): inverse = jax.scipy.linalg.cho_solve((factor, True), pivot_block.T)]
  transfers between devices with their start and end apart: 4 -> 0, of which waited for: 1 -> 0; matrix products, arithmetic and copies ran while one was open for 48% -> 0% of each run, Pallas kernels for 0% -> 0%
where the time goes in v1:
time: 86.7 us; the launch traced here: 85.7 us
  Pallas kernels  83.7 us (97%)
  local copies, waits for them, and re-layouts  1.97 us (2%)
    pallas_call x1, Pallas kernels, shards(): pl.pallas_call(route_kernel, out_shape=(jax.ShapeDtypeStruct((CB, 6, *str...  71 us
    pallas_call x1, Pallas kernels, shards(): pl.pallas_call(update_kernel, out_shape=jax.ShapeDtypeStruct(stored_tiles...  12.7 us
    unnamed x4, local copies, waits for them, and re-layouts  1.97 us

profile of v1, /device:TPU:1, one launch (start us, length us, event | category | flops | bytes accessed | tf_op | source)
XLA Modules:
  0.0 85.7 jit_solution(646706010043017842)
XLA Ops:
  0.0 0.0 copy-start
  0.0 1.3 %copy-done = f32[1,10,64,512]{3,2,1,0:T(8,128)S(1)} copy-done((f32[1,10,64,512]{3,2,1,0:T(8,128)S(1)}, f32[1,10,64,512]{3,2,1,0:T(8,128)}, u32[]{:S(2)}) %copy-start) | copy-done | bytes 1310744
  1.3 0.0 copy-start.1
  1.3 0.7 copy-done.1
  2.0 71.0 %shard_map.28 = (bf16[4,6,64,128]{3,2,1,0:T(8,128)(2,1)S(1)}, bf16[8,4,4,64,128]{4,3,2,1,0:T(8,128)(2,1)S(1)}, bf16[8,4,64,128]{3,2,1,0:T(8,128)(2,1)S(1)}) custom-call(s32[64]{0:T(128)S(1)} %copy-done.1, f32[1,10,64,512]{3,2,1,0:T(8,128)S(1)} %copy-done), custom_call_target="tpu_custom_call" | custom-call | tf_op jit(solution)/shard_map/pallas_call | solution.py:426
  73.0 12.7 %shard_map.29 = f32[1,10,64,512]{3,2,1,0:T(8,128)} custom-call(s32[64]{0:T(128)S(1)} %copy-done.1, f32[1,10,64,512]{3,2,1,0:T(8,128)S(1)} %copy-done, bf16[4,6,64,128]{3,2,1,0:T(8,128)(2,1)S(1)} %get-tuple-element.8.fin, bf16[8,4,4,64,128]{4,3,2,1,0:T(8,128)(2,1)S(1)} %get-tuple-element.9.right, bf16[8,4,64,128]{3,2,1,0:T(8,128)(2,1)S(1)} %get-tuple-element.10.piv), custom_call_target="tpu_custom_call" | custom-call | tf_op jit(solution)/shard_map/pallas_call | solution.py:467
Async XLA Ops:
  0.0 1.3 %copy-start = (f32[1,10,64,512]{3,2,1,0:T(8,128)S(1)}, f32[1,10,64,512]{3,2,1,0:T(8,128)}, u32[]{:S(2)}) copy-start(f32[1,10,64,512]{3,2,1,0:T(8,128)} %tiles_ref.3) | copy-start | bytes 3932164
  1.3 0.7 copy-start.1

commit v2 on v1

--- a/solution.py
+++ b/solution.py
@@ -65,6 +65,12 @@
     fin,
     right,
     piv,
+    xb,
+    xl,
+    size_ref,
+    p,
+    xf,
+    yv,
     loaded,
     panel,
     a2r,
@@ -225,6 +231,10 @@
     drain(gathered.at[:, 0 : 3 * PIECE], m_recv)
     for k, dy in enumerate(others4):
         send(gathered, gathered, y_send, y_recv, (lax.rem(y + dy, NY), z, x, c))
+    drain(piv.at[0:4], p_recv.at[5])
+    whole_pivot(piv, p)
+    newton_start(p, xb, yv)
+    newton_steps(p, xb, yv, 0, 1)
     drain(yb.at[0:3], y_recv)
 
     def pick(cell, out):
@@ -240,6 +250,7 @@
             msg.at[k], fin.at[res], w_send, w_recv.at[k], (y, lax.rem(z + dz, NZ), x, c)
         )
     pick(cells[0], fin.at[res])
+    newton_steps(p, xb, yv, 1, 4)
 
     for part_no in range(4):
         if part_no > 0:
@@ -255,6 +266,11 @@
                 (y, z, lax.rem(x + dx, NX), c),
             )
         send(fin.at[b, 2:6], right.at[u, b], c_send, c_recv, (y, z, x, 1 - c))
+    newton_steps(p, xb, yv, 4, 6)
+    yv[...] = jnp.where(identity(), 1.0, 0.0) - yv[...]
+    size_ref[...] = jnp.broadcast_to(jnp.sum(yv[...] * yv[...]), size_ref.shape)
+    xf[...] = xb[...].astype(F32)
+    refine(xb, xl, xf, yv)
     for part_no in range(4):
         b = lax.rem(z - (0, 1, 15, far2)[part_no] + NZ, 4)
         for k, dx in enumerate(others4):
@@ -262,7 +278,6 @@
             source = lax.rem(x - dx + NX, NX) * NC + c
             send(right.at[source, b], right.at[source, b], c_send, c_recv, (y, z, x, 1 - c))
     drain(right.at[0:4], c_recv)
-    drain(piv.at[0:4], p_recv.at[5])
 
     drain(pyr.at[0:3], p_send.at[0])
     drain(wz.at[0:3], p_send.at[1])
@@ -304,29 +319,68 @@
     return lax.broadcasted_iota(jnp.int32, shape, 0) == lax.broadcasted_iota(jnp.int32, shape, 1)
 
 
-def newton(p, xb, yv):
+COEFS = schedule(NEWTON_LOW, NEWTON_STEPS)
+
+
+def whole_pivot(piv, p):
+    for v in range(SUB):
+        for b in range(CB):
+            p[v * ROWS : (v + 1) * ROWS, b * LANES : (b + 1) * LANES] = piv[v, b]
+
+
+def newton_start(p, xb, yv):
     yv[...] = dot_nt(p[...], p[...])
     bound = jnp.max(jnp.sum(jnp.abs(yv[...]), axis=0, keepdims=True))
     inv = 1.0 / bound
     xb[...] = (p[...].astype(F32) * -inv).astype(BF)
     yv[...] = yv[...] * inv
-    coefs = schedule(NEWTON_LOW, NEWTON_STEPS)
-
+
+
+def newton_steps(p, xb, yv, lo, hi):
     def step(k, carry):
-        c1, c2 = jnp.float32(coefs[0][0]), jnp.float32(coefs[0][1])
-        for i in range(1, NEWTON_STEPS):
-            c1 = jnp.where(k == i, coefs[i][0], c1)
-            c2 = jnp.where(k == i, coefs[i][1], c2)
+        c1, c2 = jnp.float32(COEFS[lo][0]), jnp.float32(COEFS[lo][1])
+        for i in range(lo + 1, hi):
+            c1 = jnp.where(k == i, COEFS[i][0], c1)
+            c2 = jnp.where(k == i, COEFS[i][1], c2)
         m = (jnp.where(identity(), c1, 0.0) - c2 * yv[...]).astype(BF)
         xb[...] = dot(xb[...], m).astype(BF)
         yv[...] = dot(p[...], xb[...])
         return carry
 
-    lax.fori_loop(0, NEWTON_STEPS, step, 0)
+    lax.fori_loop(lo, hi, step, 0)
+
+
+def refine(xb, xl, xf, yv):
+    small = yv[...].astype(BF)
+    yv[...] = yv[...] + dot(small, small)
+    better = xf[...] + dot(xf[...].astype(BF), yv[...].astype(BF))
+    high = better.astype(BF)
+    xb[...] = high
+    xl[...] = (better - high.astype(F32)).astype(BF)
 
 
 def update_kernel(
-    owner_ref, tiles_ref, fin, right, piv, out_ref, cur, p, xb, xf, yv, rt, left, in_sem, out_sem
+    owner_ref,
+    tiles_ref,
+    fin,
+    right,
+    xb_in,
+    xl_in,
+    size_ref,
+    piv_any,
+    out_ref,
+    cur,
+    xb,
+    xl,
+    p,
+    piv,
+    xf,
+    yv,
+    rt,
+    left,
+    in_sem,
+    out_sem,
+    piv_sem,
 ):
     for slot in range(10):
         pltpu.make_async_copy(tiles_ref.at[0, slot], cur.at[slot], in_sem.at[slot]).start()
@@ -334,49 +388,40 @@
     (cell,) = cells_at(owner_ref, (me,))
     row_group, col_group, first = groups_of(cell)
     diagonal = row_group == col_group
-
-    for v in range(SUB):
-        for b in range(CB):
-            p[v * ROWS : (v + 1) * ROWS, b * LANES : (b + 1) * LANES] = piv[v, b]
-    newton(p, xb, yv)
-
-    yv[...] = jnp.where(identity(), 1.0, 0.0) - yv[...]
-    xf[...] = xb[...].astype(F32)
-    highest = lax.Precision.HIGHEST
-    size = jnp.sum(yv[...] * yv[...])
-
-    @pl.when(jnp.logical_not(size < 0.01))
+    good = jnp.max(size_ref[...]) < 0.01
+
+    @pl.when(good)
     def _():
-        @pl.when(jnp.logical_not(size < 0.25))
-        def _():
-            whole = p[...].astype(F32)
-            rows = jnp.max(jnp.sum(jnp.abs(whole), axis=0, keepdims=True))
-            xf[...] = whole * (-1.0 / rows) / rows
+        xb[...] = xb_in[...]
+        xl[...] = xl_in[...]
+
+    @pl.when(jnp.logical_not(good))
+    def _():
+        copy = pltpu.make_async_copy(piv_any, piv, piv_sem)
+        copy.start()
+        copy.wait()
+        whole_pivot(piv, p)
+        highest = lax.Precision.HIGHEST
+        whole = p[...].astype(F32)
+        rows = jnp.max(jnp.sum(jnp.abs(whole), axis=0, keepdims=True))
+        xf[...] = whole * (-1.0 / rows) / rows
 
         def residual():
-            yv[...] = jnp.where(identity(), 1.0, 0.0) - dot(
-                p[...].astype(F32), xf[...], highest
-            )
+            yv[...] = jnp.where(identity(), 1.0, 0.0) - dot(p[...].astype(F32), xf[...], highest)
             return jnp.sum(yv[...] * yv[...])
 
         def more(carry):
-            k, size = carry
+            k, _ = carry
             xf[...] = xf[...] + dot(xf[...], yv[...], highest)
             return k + 1, residual()
 
         lax.while_loop(lambda s: (s[0] < 150) & (s[1] > 0.001), more, (0, residual()))
-
-    small = yv[...].astype(BF)
-    yv[...] = yv[...] + dot(small, small)
-    xf[...] = xf[...] + dot(xf[...].astype(BF), yv[...].astype(BF))
-
-    high = xf[...].astype(BF)
-    xb[...] = high
-    xf[...] = xf[...] - high.astype(F32)
+        refine(xb, xl, xf, yv)
+
     for i in range(PER):
         strip = jnp.concatenate([fin[b, i] for b in range(CB)], axis=1)
         left[i * ROWS : (i + 1) * ROWS] = (
-            dot(strip, xb[...]) + dot(strip, xf[...].astype(BF))
+            dot(strip, xb[...]) + dot(strip, xl[...])
         ).astype(BF)
 
     def stage(j, strip):
@@ -423,16 +468,25 @@
     smem = pl.BlockSpec(memory_space=pltpu.SMEM)
     hbm = pl.BlockSpec(memory_space=pl.ANY)
     strip = (ROWS, LANES)
-    fin, right, piv = pl.pallas_call(
+    stored_tiles = pltpu.with_memory_space_constraint(stored_tiles, pltpu.HBM)
+    square = pltpu.VMEM((N, N), BF)
+    square32 = pltpu.VMEM((N, N), F32)
+    fin, right, piv, xb, xl, size = pl.pallas_call(
         route_kernel,
         out_shape=(
             jax.ShapeDtypeStruct((CB, 6, *strip), BF),
             jax.ShapeDtypeStruct((SUB, CB, 4, *strip), BF),
             jax.ShapeDtypeStruct((SUB, CB, *strip), BF),
+            jax.ShapeDtypeStruct((N, N), BF),
+            jax.ShapeDtypeStruct((N, N), BF),
+            jax.ShapeDtypeStruct((8, LANES), F32),
         ),
         in_specs=[smem, hbm],
-        out_specs=(vmem, vmem, vmem),
+        out_specs=(vmem, vmem, vmem, vmem, vmem, vmem),
         scratch_shapes=[
+            square,
+            square32,
+            square32,
             pltpu.VMEM((len(LOAD_SLOTS), ROWS, N), F32),
             pltpu.VMEM((PER, CB, *strip), BF),
             pltpu.VMEM((TRI, PIECE, LANES), BF),
@@ -467,21 +521,24 @@
     return pl.pallas_call(
         update_kernel,
         out_shape=jax.ShapeDtypeStruct(stored_tiles.shape, F32),
-        in_specs=[smem, hbm, vmem, vmem, vmem],
+        in_specs=[smem, hbm, vmem, vmem, vmem, vmem, vmem, hbm],
         out_specs=hbm,
         scratch_shapes=[
             pltpu.VMEM((10, ROWS, N), F32),
-            pltpu.VMEM((N, N), BF),
-            pltpu.VMEM((N, N), BF),
-            pltpu.VMEM((N, N), F32),
-            pltpu.VMEM((N, N), F32),
+            square,
+            square,
+            square,
+            pltpu.VMEM((SUB, CB, *strip), BF),
+            square32,
+            square32,
             pltpu.VMEM((PER, N, N), BF),
             pltpu.VMEM((PER * ROWS, N), BF),
             dma((10,)),
             dma((10,)),
+            dma,
         ],
         compiler_params=pltpu.CompilerParams(vmem_limit_bytes=40 * 2**20),
-    )(cell_owner, stored_tiles, fin, right, piv)
+    )(cell_owner, stored_tiles, fin, right, xb, xl, size, piv)
 
 
 def solution(mesh):

time: 86.7 us -> 77 us (0.89); the launches traced: 85.7 us -> 76.9 us
  Pallas kernels: 83.7 us -> 76.3 us
  local copies, waits for them, and re-layouts: 1.97 us -> 0.65 us
    pallas_call x1, Pallas kernels: 12.7 us -> 4.16 us  [shards(): pl.pallas_call(update_kernel, out_shape=jax.ShapeDtypeStruct(stored_tiles...]
    unnamed x4 -> x2, local copies, waits for them, and re-layouts: 1.97 us -> 0.65 us
    pallas_call x1, Pallas kernels: 71 us -> 72.1 us  [shards(): pl.pallas_call(route_kernel, out_shape=(jax.ShapeDtypeStruct((CB, 6, *str...]
where the time goes in v2:
time: 77 us; the launch traced here: 76.9 us
  Pallas kernels  76.3 us (99%)
    pallas_call x1, Pallas kernels, shards(): pl.pallas_call(route_kernel, out_shape=(jax.ShapeDtypeStruct((CB, 6, *str...  72.1 us
    pallas_call x1, Pallas kernels, shards(): pl.pallas_call(update_kernel, out_shape=jax.ShapeDtypeStruct(stored_tiles...  4.16 us

profile of v2, /device:TPU:1, one launch (start us, length us, event | category | flops | bytes accessed | tf_op | source)
XLA Modules:
  0.0 76.9 jit_solution(9481562495876135330)
XLA Ops:
  0.0 0.0 copy-start
  0.0 0.7 copy-done
  0.7 72.1 %shard_map.28 = (bf16[4,6,64,128]{3,2,1,0:T(8,128)(2,1)S(1)}, bf16[8,4,4,64,128]{4,3,2,1,0:T(8,128)(2,1)S(1)}, bf16[8,4,64,128]{3,2,1,0:T(8,128)(2,1)S(1)}, bf16...) custom-call(s32[64]{0:T(128)S(1)} %copy-done, f32[1,10,64,512]{3,2,1,0:T(8,128)} %tiles_ref.3), custom_call_target="tpu_custom_call" | custom-call | tf_op jit(solution)/shard_map/pallas_call | solution.py:474
  72.8 4.2 %shard_map.29 = f32[1,10,64,512]{3,2,1,0:T(8,128)} custom-call(s32[64]{0:T(128)S(1)} %copy-done, f32[1,10,64,512]{3,2,1,0:T(8,128)} %tiles_ref.3, bf16[4,6,64,128]{3,2,1,0:T(8,128)(2,1)S(1)} %get-tuple-element.11.fin, bf16[8,4,4,64,128]{4,3,2,1,0:T(8,128)(2,1)S(1)} %get-tuple-element.12.right, bf16[512,512]{1,0:T(8,128)(2,1)S(1)} %get-tuple-element.13.xb_in, ...), custom_call_target="tpu_custom_call" | custom-call | tf_op jit(solution)/shard_map/pallas_call | solution.py:521
Async XLA Ops:
  0.0 0.7 copy-start

commit v3 on v0

v3 whole, which is shorter than its diff:
```python
import jax
import jax.numpy as jnp
from jax import lax
from jax.experimental import pallas as pl
from jax.experimental.pallas import tpu as pltpu
from jax.sharding import Mesh
from jax.sharding import PartitionSpec as P

MESH = pl.DeviceIdType.MESH
AXES = ("y", "z", "x", "c")
NY, NZ, NX, NC = 4, 16, 4, 2
TRI = NY * NZ
SUB = NX * NC
GROUPS = 8
PER = 4
SLOTS = 10
N = 512
ROWS = N // SUB
LANES = 128
CB = N // LANES
PIECE = 16
LOAD_SLOTS = (0, 1, 2, 3, 4, 6)
FIRST_SLOTS = (0, 1, 3, 6)
PAIRS = tuple((i, j) for i in range(PER) for j in range(i + 1))
NEWTON_STEPS = 6
NEWTON_LOW = 0.004
SMALL = 0.01
BF = jnp.bfloat16
F32 = jnp.float32


def drain(ref, sem):
    pltpu.make_async_copy(ref, ref, sem).wait()


def send(src, dst, send_sem, recv_sem, device):
    pltpu.make_async_remote_copy(
        src_ref=src,
        dst_ref=dst,
        send_sem=send_sem,
        recv_sem=recv_sem,
        device_id=device,
        device_id_type=MESH,
    ).start()


def cells_at(owner_ref, places):
    def body(c, found):
        owner = owner_ref[c]
        return tuple(jnp.where(owner == t, c, f) for t, f in zip(places, found))

    zero = jnp.int32(0)
    return lax.fori_loop(0, TRI, body, tuple(zero for _ in places))


def groups_of(cell):
    down = lax.shift_right_logical(cell, jnp.int32(3))
    across = lax.bitwise_and(cell, jnp.int32(7))
    first = jnp.where(down < across, 2, 0)
    return jnp.maximum(down, across), jnp.minimum(down, across), first


def dot(a, b, precision=None):
    return lax.dot_general(
        a, b, (((1,), (0,)), ((), ())), precision=precision, preferred_element_type=F32
    )


def dot_nt(a, b):
    return lax.dot_general(a, b, (((1,), (1,)), ((), ())), preferred_element_type=F32)


def schedule(low, steps):
    out, scale = [], 1.0
    for _ in range(steps):
        s = (1 + low) / (1 - low)
        t = 2 * s * s - 1
        out.append((8 * (1 + low) / (1 - low) ** 2 / t / scale, 8 / (1 - low) ** 2 / t / scale**2))
        scale, low = 1 + 1 / t, (1 - 1 / t) / (1 + 1 / t)
    return out


COEFS = schedule(NEWTON_LOW, NEWTON_STEPS)


def identity():
    shape = (N, N)
    return lax.broadcasted_iota(jnp.int32, shape, 0) == lax.broadcasted_iota(jnp.int32, shape, 1)


def whole_pivot(piv, p):
    for v in range(SUB):
        for b in range(CB):
            p[v * ROWS : (v + 1) * ROWS, b * LANES : (b + 1) * LANES] = piv[v, b]


def newton_start(p, xb, yv):
    yv[...] = dot_nt(p[...], p[...])
    bound = jnp.max(jnp.sum(jnp.abs(yv[...]), axis=0, keepdims=True))
    inv = 1.0 / bound
    xb[...] = (p[...].astype(F32) * -inv).astype(BF)
    yv[...] = yv[...] * inv


def newton_steps(p, xb, yv, lo, hi):
    def step(k, carry):
        c1, c2 = jnp.float32(COEFS[lo][0]), jnp.float32(COEFS[lo][1])
        for i in range(lo + 1, hi):
            c1 = jnp.where(k == i, COEFS[i][0], c1)
            c2 = jnp.where(k == i, COEFS[i][1], c2)
        m = (jnp.where(identity(), c1, 0.0) - c2 * yv[...]).astype(BF)
        xb[...] = dot(xb[...], m).astype(BF)
        yv[...] = dot(p[...], xb[...])
        return carry

    lax.fori_loop(lo, hi, step, 0)


def refine(xb, xl, xf, yv):
    small = yv[...].astype(BF)
    yv[...] = yv[...] + dot(small, small)
    better = xf[...] + dot(xf[...].astype(BF), yv[...].astype(BF))
    high = better.astype(BF)
    xb[...] = high
    xl[...] = (better - high.astype(F32)).astype(BF)


def scale_rows(fin, xb, xl, left):
    for i in range(PER):
        strip = jnp.concatenate([fin[b, 0, i] for b in range(CB)], axis=1)
        left[i * ROWS : (i + 1) * ROWS] = (dot(strip, xb[...]) + dot(strip, xl[...])).astype(BF)


def products(left, right, rt, us):
    for j in range(PER):
        for v in range(SUB):
            for b in range(CB):
                rt[v * ROWS : (v + 1) * ROWS, b * LANES : (b + 1) * LANES] = right[v, b, j]
        product = dot_nt(left[...], rt[...])
        for i in range(PER):
            us[j, i] = product[i * ROWS : (i + 1) * ROWS]


def add_products(cell, us, cur, slot):
    row_group, col_group, first = groups_of(cell)
    diagonal = row_group == col_group
    i, j = PAIRS[slot]
    half = min(slot, 7)
    i = jnp.where(diagonal, i, half // 2)
    j = jnp.where(diagonal, j, first + half % 2)
    live = (col_group > 0) | (j > 0)
    if slot > 7:
        live = live & diagonal
    cur[slot] = cur[slot] + jnp.where(live, us[j, i], 0.0)


def route_kernel(
    owner_ref,
    tiles_ref,
    upd,
    size_ref,
    fin_out,
    right_out,
    piv_out,
    cur,
    panel,
    a2r,
    gath0,
    gath1,
    gath2,
    gath3,
    msg,
    fin,
    right,
    piv,
    wz,
    mz,
    p,
    xb,
    xl,
    xf,
    yv,
    left,
    rt,
    us,
    load_sem,
    p_send,
    p_recv,
    a_send,
    a_recv,
    m_send,
    m_recv,
    w_send,
    w_recv,
    x_send,
    x_recv,
    c_send,
    c_recv,
    q_send,
    q_recv,
    o_sem,
    k_sem,
):
    y, z = lax.axis_index("y"), lax.axis_index("z")
    x, c = lax.axis_index("x"), lax.axis_index("c")
    me = y * NZ + z
    u = x * NC + c
    res = lax.rem(z, 4)
    quo = z // 4
    far2 = 2 + 12 * c
    window = (0, 1, 15, far2)
    mates = (0, 4, 12, 8)
    others4 = (2, 1, 3)
    gath = (gath0, gath1, gath2, gath3)
    near = [(dy, k) for k in range(4) for dy in (2, 1, 3, 0) if (dy, k) != (0, 0)]
    sibling = (y, z, x, 1 - c)

    def at_tri(dy, dz):
        return (lax.rem(y + dy, NY), lax.rem(z + dz, NZ), x, c)

    def at_x(dx):
        return (y, z, lax.rem(x + dx, NX), c)

    def from_x(dx):
        return lax.rem(x - dx + NX, NX) * NC + c

    for slot in LOAD_SLOTS:
        pltpu.make_async_copy(tiles_ref.at[0, slot], cur.at[slot], load_sem.at[slot]).start()

    barrier = pltpu.get_barrier_semaphore()

    def greet(k, carry):
        pl.semaphore_signal(
            barrier, inc=1, device_id=at_tri(k // NZ, lax.rem(k, NZ)), device_id_type=MESH
        )
        return carry

    lax.fori_loop(1, TRI, greet, 0)
    for d in others4:
        pl.semaphore_signal(barrier, inc=1, device_id=at_x(d), device_id_type=MESH)
    pl.semaphore_signal(barrier, inc=1, device_id=sibling, device_id_type=MESH)
    for slot in range(SLOTS):
        if slot not in LOAD_SLOTS:
            pltpu.make_async_copy(tiles_ref.at[0, slot], cur.at[slot], load_sem.at[slot]).start()

    (cell,) = cells_at(owner_ref, (me,))
    pivot_at = owner_ref[0]
    y0 = lax.shift_right_logical(pivot_at, jnp.int32(4))
    z0 = lax.bitwise_and(pivot_at, jnp.int32(15))
    for slot in LOAD_SLOTS:
        pltpu.make_async_copy(tiles_ref.at[0, slot], cur.at[slot], load_sem.at[slot]).wait()
    is_first = cell < GROUPS
    for i in range(PER):
        tile = jnp.where(is_first, cur[FIRST_SLOTS[i]], cur[2 * i]).astype(BF)
        for b in range(CB):
            panel[i, b] = tile[:, b * LANES : (b + 1) * LANES]
    cells = {(0, 0): cell}
    found = cells_at(owner_ref, tuple(
        lax.rem(y + dy, NY) * NZ + lax.rem(z + window[k], NZ) for dy, k in near
    ))
    cells.update(zip(near, found))
    pl.semaphore_wait(barrier, TRI - 1 + 4)

    my_row = pl.multiple_of(quo * PIECE, PIECE)
    res_row = pl.multiple_of(res * PIECE, PIECE)
    for dy, k in near:
        ty, tz, _, _ = at_tri(dy, window[k])
        row = pl.multiple_of(lax.rem(tz, 4) * PIECE, PIECE)
        send(
            panel.at[0, ty, pl.ds(row, PIECE)],
            wz.at[dy * 4 + k],
            p_send.at[0],
            p_recv.at[0],
            (ty, tz, x, c),
        )
    wz[0] = panel[0, y, pl.ds(res_row, PIECE)]

    def spread(dy, dz):
        ty, tz, _, _ = at_tri(dy, dz)
        row = pl.multiple_of((tz // 4) * PIECE, PIECE)
        send(
            panel.at[ty, lax.rem(tz, 4), pl.ds(row, PIECE)],
            a2r.at[me],
            a_send,
            a_recv,
            (ty, tz, x, c),
        )

    def spread_all(k, carry):
        spread(k // NZ, lax.rem(k, NZ))
        return carry

    lax.fori_loop(1, TRI, spread_all, 0)
    a2r[me] = panel[y, res, pl.ds(my_row, PIECE)]

    def near_to(delta):
        return (delta == 0) | (delta == 1) | (delta == 15) | (delta == far2)

    drain(wz.at[1:16], p_recv.at[0])
    delta = lax.bitwise_and(z - z0, 15)
    came = jnp.where(delta == 1, 1, jnp.where(delta == 15, 2, jnp.where(delta == far2, 3, 0)))
    mz[0] = wz[lax.bitwise_and(y - y0, 3) * 4 + came]
    for k in range(1, 4):
        send(mz.at[0], mz.at[k], p_send.at[1], p_recv.at[1], at_tri(0, mates[k]))
    drain(mz.at[1:4], p_recv.at[1])
    came = jnp.int32(0)
    for k in range(1, 4):
        delta = lax.bitwise_and(z - mates[k] - z0, 15)
        came = jnp.where(near_to(delta), k, came)
    part = piv.at[u, y, pl.ds(res_row, PIECE)]
    part[...] = mz[came]
    for dy, k in near:
        send(part, part, p_send.at[2], p_recv.at[2], at_tri(dy, window[k]))

    drain(a2r.at[0 : TRI - 1], a_recv)
    for g in range(GROUPS):
        gath0[g] = a2r[owner_ref[g * GROUPS]]
    for k in (3, 1, 2):
        send(gath0, gath[k], m_send, m_recv.at[k], at_tri(0, mates[k]))

    def row_of(place):
        return pl.multiple_of((lax.rem(place + 2 * NZ, NZ) // 4) * PIECE, PIECE)

    def hand_out(q):
        row = row_of(z - mates[q])
        for n, (dy, k) in enumerate(near):
            row_group, col_group, _ = groups_of(cells[dy, k])
            msg[q, n, 0] = gath[q][row_group]
            msg[q, n, 1] = gath[q][col_group]
            send(
                msg.at[q, n],
                fin.at[res, :, y, pl.ds(row, PIECE)],
                w_send,
                w_recv.at[q, k],
                at_tri(dy, window[k]),
            )
        row_group, col_group, _ = groups_of(cell)
        fin[res, 0, y, pl.ds(row, PIECE)] = gath[q][row_group]
        fin[res, 1, y, pl.ds(row, PIECE)] = gath[q][col_group]

    def part_of(q, k):
        source = z - window[k]
        b = lax.rem(source + NZ, 4)
        return b, row_of(source - mates[q])

    def over_x(q):
        for k in range(4):
            drain(msg.at[0, 0 : 3 if k == 0 else 4], w_recv.at[q, k])
            b, row = part_of(q, k)
            rows = pl.ds(row, PIECE)
            for n, dx in enumerate(others4):
                send(
                    fin.at[b, 1, :, rows],
                    right.at[u, b, :, rows],
                    x_send,
                    x_recv.at[q, n],
                    at_x(dx),
                )
            send(fin.at[b, 1, :, rows], right.at[u, b, :, rows], c_send, c_recv, sibling)

    def over_core(q):
        for n in (1, 2, 0):
            drain(right.at[0, :, :, 0:PIECE], x_recv.at[q, n])
            source = from_x(others4[n])
            for k in range(4):
                b, row = part_of(q, k)
                there = right.at[source, b, :, pl.ds(row, PIECE)]
                send(there, there, c_send, c_recv, sibling)

    hand_out(0)
    drain(wz.at[1:16], p_recv.at[2])
    strip = piv.at[u]
    for n, dx in enumerate(others4):
        send(strip, strip, p_send.at[3], q_recv.at[n], at_x(dx))
    send(strip, strip, q_send, p_recv.at[3], sibling)
    for q in (1, 2):
        drain(gath[q], m_recv.at[q])
        hand_out(q)
    over_x(0)
    for n in (1, 2, 0):
        drain(strip, q_recv.at[n])
        there = piv.at[from_x(others4[n])]
        send(there, there, q_send, p_recv.at[3], sibling)
    drain(gath[3], m_recv.at[3])
    hand_out(3)
    drain(piv.at[0:4], p_recv.at[3])
    whole_pivot(piv, p)
    keep_piv = pltpu.make_async_copy(piv, piv_out, k_sem.at[0])
    keep_piv.start()
    newton_start(p, xb, yv)
    over_x(1)
    over_x(2)
    newton_steps(p, xb, yv, 0, 2)
    over_core(0)
    over_x(3)
    for b in range(CB):
        right[u, b] = fin[b, 1]
    keep_fin = pltpu.make_async_copy(fin, fin_out, k_sem.at[1])
    keep_fin.start()
    newton_steps(p, xb, yv, 2, 4)
    over_core(1)
    over_core(2)
    newton_steps(p, xb, yv, 4, 6)
    over_core(3)

    yv[...] = jnp.where(identity(), 1.0, 0.0) - yv[...]
    size_ref[...] = jnp.broadcast_to(jnp.sum(yv[...] * yv[...]), size_ref.shape)
    xf[...] = xb[...].astype(F32)
    refine(xb, xl, xf, yv)
    scale_rows(fin, xb, xl, left)

    drain(right.at[0:4], c_recv)
    keep_right = pltpu.make_async_copy(right, right_out, k_sem.at[2])
    keep_right.start()
    products(left, right, rt, us)
    for slot in range(SLOTS):
        if slot not in LOAD_SLOTS:
            pltpu.make_async_copy(tiles_ref.at[0, slot], cur.at[slot], load_sem.at[slot]).wait()
        add_products(cell, us, cur, slot)
        pltpu.make_async_copy(cur.at[slot], upd.at[0, slot], o_sem.at[slot]).start()

    drain(wz.at[1:16], p_send.at[0])
    drain(mz.at[1:4], p_send.at[1])
    drain(wz.at[1:16], p_send.at[2])
    drain(piv.at[0:3], p_send.at[3])
    drain(piv.at[0:4], q_send)
    drain(a2r.at[0 : TRI - 1], a_send)
    drain(a2r.at[0 : 3 * GROUPS], m_send)
    drain(msg, w_send)
    drain(right.at[0:3], x_send)
    drain(right.at[0:4], c_send)
    keep_piv.wait()
    keep_fin.wait()
    keep_right.wait()
    for slot in range(SLOTS):
        pltpu.make_async_copy(cur.at[slot], upd.at[0, slot], o_sem.at[slot]).wait()


def result_kernel(
    size_ref,
    owner_any,
    tiles_ref,
    upd,
    fin_any,
    right_any,
    piv_any,
    out_ref,
    owner_ref,
    cur,
    fin,
    right,
    piv,
    p,
    xb,
    xl,
    xf,
    yv,
    left,
    rt,
    us,
    sem,
    out_sem,
):
    good = jnp.max(size_ref[...]) < SMALL

    @pl.when(good)
    def _():
        for slot in range(SLOTS):
            pltpu.make_async_copy(upd.at[0, slot], out_ref.at[0, slot], out_sem.at[slot]).start()
        for slot in range(SLOTS):
            pltpu.make_async_copy(upd.at[0, slot], out_ref.at[0, slot], out_sem.at[slot]).wait()

    @pl.when(jnp.logical_not(good))
    def _():
        pairs = (
            (owner_any, owner_ref),
            (tiles_ref.at[0], cur),
            (fin_any, fin),
            (right_any, right),
            (piv_any, piv),
        )
        for n, (src, dst) in enumerate(pairs):
            copy = pltpu.make_async_copy(src, dst, sem.at[n])
            copy.start()
            copy.wait()
        me = lax.axis_index("y") * NZ + lax.axis_index("z")
        (cell,) = cells_at(owner_ref, (me,))
        whole_pivot(piv, p)
        highest = lax.Precision.HIGHEST
        whole = p[...].astype(F32)
        rows = jnp.max(jnp.sum(jnp.abs(whole), axis=0, keepdims=True))
        xf[...] = whole * (-1.0 / rows) / rows

        def residual():
            yv[...] = jnp.where(identity(), 1.0, 0.0) - dot(p[...].astype(F32), xf[...], highest)
            return jnp.sum(yv[...] * yv[...])

        def more(carry):
            k, _ = carry
            xf[...] = xf[...] + dot(xf[...], yv[...], highest)
            return k + 1, residual()

        lax.while_loop(lambda s: (s[0] < 150) & (s[1] > 0.001), more, (0, residual()))
        refine(xb, xl, xf, yv)
        scale_rows(fin, xb, xl, left)
        products(left, right, rt, us)
        for slot in range(SLOTS):
            add_products(cell, us, cur, slot)
            copy = pltpu.make_async_copy(cur.at[slot], out_ref.at[0, slot], out_sem.at[slot])
            copy.start()
            copy.wait()


def shards(stored_tiles, cell_owner):
    dma = pltpu.SemaphoreType.DMA
    vmem = pl.BlockSpec(memory_space=pltpu.VMEM)
    anywhere = pl.BlockSpec(memory_space=pl.ANY)
    hbm = pl.BlockSpec(memory_space=pltpu.HBM)
    strip = (ROWS, LANES)
    fin_shape = (CB, 2, PER, *strip)
    right_shape = (SUB, CB, PER, *strip)
    piv_shape = (SUB, CB, *strip)
    work = [
        pltpu.VMEM((N, N), BF),
        pltpu.VMEM((N, N), BF),
        pltpu.VMEM((N, N), BF),
        pltpu.VMEM((N, N), F32),
        pltpu.VMEM((N, N), F32),
        pltpu.VMEM((PER * ROWS, N), BF),
        pltpu.VMEM((N, N), BF),
        pltpu.VMEM((PER, PER, ROWS, N), F32),
    ]
    owner = pltpu.SMEM((TRI,), jnp.int32)
    stored_tiles = pltpu.with_memory_space_constraint(stored_tiles, pltpu.HBM)
    tiles = pltpu.VMEM((SLOTS, ROWS, N), F32)
    upd, size, fin, right, piv = pl.pallas_call(
        route_kernel,
        out_shape=(
            jax.ShapeDtypeStruct(stored_tiles.shape, F32),
            jax.ShapeDtypeStruct((8, LANES), F32),
            jax.ShapeDtypeStruct(fin_shape, BF),
            jax.ShapeDtypeStruct(right_shape, BF),
            jax.ShapeDtypeStruct(piv_shape, BF),
        ),
        in_specs=[pl.BlockSpec(memory_space=pltpu.SMEM), hbm],
        out_specs=(anywhere, vmem, hbm, hbm, hbm),
        scratch_shapes=[
            tiles,
            pltpu.VMEM((PER, CB, *strip), BF),
            pltpu.VMEM((TRI, PIECE, LANES), BF),
            pltpu.VMEM((GROUPS, PIECE, LANES), BF),
            pltpu.VMEM((GROUPS, PIECE, LANES), BF),
            pltpu.VMEM((GROUPS, PIECE, LANES), BF),
            pltpu.VMEM((GROUPS, PIECE, LANES), BF),
            pltpu.VMEM((4, 15, 2, PIECE, LANES), BF),
            pltpu.VMEM(fin_shape, BF),
            pltpu.VMEM(right_shape, BF),
            pltpu.VMEM(piv_shape, BF),
            pltpu.VMEM((16, PIECE, LANES), BF),
            pltpu.VMEM((4, PIECE, LANES), BF),
            *work,
            dma((SLOTS,)),
            dma((4,)),
            dma((4,)),
            dma,
            dma,
            dma,
            dma((4,)),
            dma,
            dma((4, 4)),
            dma,
            dma((4, 3)),
            dma,
            dma,
            dma,
            dma((3,)),
            dma((SLOTS,)),
            dma((3,)),
        ],
        compiler_params=pltpu.CompilerParams(
            collective_id=0, has_side_effects=True, vmem_limit_bytes=48 * 2**20
        ),
    )(cell_owner, stored_tiles)
    return pl.pallas_call(
        result_kernel,
        out_shape=jax.ShapeDtypeStruct(stored_tiles.shape, F32),
        in_specs=[vmem, anywhere, hbm, anywhere, hbm, hbm, hbm],
        out_specs=hbm,
        scratch_shapes=[
            owner,
            tiles,
            pltpu.VMEM(fin_shape, BF),
            pltpu.VMEM(right_shape, BF),
            pltpu.VMEM(piv_shape, BF),
            *work,
            dma((5,)),
            dma((SLOTS,)),
        ],
        compiler_params=pltpu.CompilerParams(vmem_limit_bytes=40 * 2**20),
    )(size, cell_owner, stored_tiles, upd, fin, right, piv)


def solution(mesh):
    torus = Mesh(mesh.devices.reshape(NY, NZ, NX, NC), AXES)
    spec = P(("y", "z"), None, ("x", "c"), None)
    return jax.shard_map(
        shards, mesh=torus, in_specs=(spec, P()), out_specs=spec, check_vma=False
    )
```

time: 329 us -> 68.3 us (0.21); the launches traced: 323 us -> 68.1 us
  other arithmetic: 129 us -> 0 us
  Pallas kernels: 0 us -> 67.3 us
  blocking collectives: 66.1 us -> 0 us
  starting transfers between devices: 34.3 us -> 0 us
  local copies, waits for them, and re-layouts: 34.8 us -> 0.65 us
  between operations: 21.8 us -> 0.19 us
  waiting for transfers between devices: 21.6 us -> 0 us
  matrix products: 16.1 us -> 0 us
    another operation x18 -> x0, other arithmetic: 119 us -> none  [the longest x14 78.7 us: shards(): factor = jnp.linalg.cholesky(gram_matrix)]
    pallas_call x0 -> x2, Pallas kernels: none -> 67.3 us  [the longest x1 66 us: shards(): pl.pallas_call(route_kernel, out_shape=(jax.ShapeDtypeStruct(stored_tiles...]
    all_gather x4 -> x0, blocking collectives: 66.1 us -> none  [the longest x3 42.5 us: gather_in_order(): tiles = lax.all_gather(tiles, axes[k], axis=0, tiled=True)]
    all_to_all x2 -> x0, starting transfers between devices: 33.9 us -> none  [the longest x1 19.3 us: shards(): lax.all_to_all(pivot_part.astype(jnp.bfloat16), TRI, split_axis=0, concat...]
    all_gather x2 -> x0, waiting for transfers between devices: 21.5 us -> none  [the longest x1 21.5 us: shards(): partner = lax.all_gather(other_strips, 'sub', axis=1, tiled=True)]
    another operation x18 -> x0, local copies, waits for them, and re-layouts: 13.6 us -> none
    gather x6 -> x0, local copies, waits for them, and re-layouts: 11.7 us -> none  [the longest x1 5.44 us: shards(): right_slots = partner[col_local]]
    another operation x20 -> x0, matrix products: 8.78 us -> none  [the longest x14 6.91 us: shards(): inverse = jax.scipy.linalg.cho_solve((factor, True), pivot_block.T)]
  transfers between devices with their start and end apart: 4 -> 0, of which waited for: 1 -> 0; matrix products, arithmetic and copies ran while one was open for 48% -> 0% of each run, Pallas kernels for 0% -> 0%
where the time goes in v3:
time: 68.3 us; the launch traced here: 68.1 us
  Pallas kernels  67.3 us (99%)
    pallas_call x1, Pallas kernels, shards(): pl.pallas_call(route_kernel, out_shape=(jax.ShapeDtypeStruct(stored_tiles...  66 us

profile of v3, /device:TPU:1, one launch (start us, length us, event | category | flops | bytes accessed | tf_op | source)
XLA Modules:
  0.0 68.1 jit_solution(263910471191040846)
XLA Ops:
  0.0 0.0 copy-start
  0.0 0.7 copy-done
  0.7 66.0 %shard_map.28 = (f32[1,10,64,512]{3,2,1,0:T(8,128)S(1)}, f32[8,128]{1,0:T(8,128)S(1)}, bf16[4,2,4,64,128]{4,3,2,1,0:T(8,128)(2,1)S(1)}, bf16[8,4,4,64,128]{4,3,2...) custom-call(s32[64]{0:T(128)S(1)} %copy-done, f32[1,10,64,512]{3,2,1,0:T(8,128)} %tiles_ref.3), custom_call_target="tpu_custom_call" | custom-call | tf_op jit(solution)/shard_map/pallas_call | solution.py:536
  66.7 1.3 %shard_map.29 = f32[1,10,64,512]{3,2,1,0:T(8,128)} custom-call(f32[8,128]{1,0:T(8,128)S(1)} %get-tuple-element.10.size_ref, s32[64]{0:T(128)S(1)} %copy-done, f32[1,10,64,512]{3,2,1,0:T(8,128)} %tiles_ref.3, f32[1,10,64,512]{3,2,1,0:T(8,128)S(1)} %get-tuple-element.11.upd, bf16[4,2,4,64,128]{4,3,2,1,0:T(8,128)(2,1)S(1)} %get-tuple-element.12.fin_any, ...), custom_call_target="tpu_custom_call" | custom-call | tf_op jit(solution)/shard_map/pallas_call | solution.py:584
Async XLA Ops:
  0.0 0.7 copy-start

commit v4 on v3

--- a/solution.py
+++ b/solution.py
@@ -22,8 +22,8 @@
 LOAD_SLOTS = (0, 1, 2, 3, 4, 6)
 FIRST_SLOTS = (0, 1, 3, 6)
 PAIRS = tuple((i, j) for i in range(PER) for j in range(i + 1))
-NEWTON_STEPS = 6
-NEWTON_LOW = 0.004
+NEWTON_STEPS = 5
+NEWTON_LOW = 0.02
 SMALL = 0.01
 BF = jnp.bfloat16
 F32 = jnp.float32
@@ -387,11 +387,12 @@
     whole_pivot(piv, p)
     keep_piv = pltpu.make_async_copy(piv, piv_out, k_sem.at[0])
     keep_piv.start()
+    over_x(1)
     newton_start(p, xb, yv)
-    over_x(1)
     over_x(2)
-    newton_steps(p, xb, yv, 0, 2)
+    newton_steps(p, xb, yv, 0, 1)
     over_core(0)
+    newton_steps(p, xb, yv, 1, 2)
     over_x(3)
     for b in range(CB):
         right[u, b] = fin[b, 1]
@@ -400,7 +401,7 @@
     newton_steps(p, xb, yv, 2, 4)
     over_core(1)
     over_core(2)
-    newton_steps(p, xb, yv, 4, 6)
+    newton_steps(p, xb, yv, 4, 5)
     over_core(3)
 
     yv[...] = jnp.where(identity(), 1.0, 0.0) - yv[...]
@@ -532,6 +533,7 @@
     ]
     owner = pltpu.SMEM((TRI,), jnp.int32)
     stored_tiles = pltpu.with_memory_space_constraint(stored_tiles, pltpu.HBM)
+    cell_owner = pltpu.with_memory_space_constraint(cell_owner, pltpu.HBM)
     tiles = pltpu.VMEM((SLOTS, ROWS, N), F32)
     upd, size, fin, right, piv = pl.pallas_call(
         route_kernel,

time: 68.3 us -> 66.9 us (0.980)
  Pallas kernels: 67.3 us -> 66.6 us
    pallas_call x1, Pallas kernels: 66 us -> 65.3 us  [shards(): pl.pallas_call(route_kernel, out_shape=(jax.ShapeDtypeStruct(stored_tiles...]
where the time goes in v4:
time: 66.9 us; the launch traced here: 66.8 us
  Pallas kernels  66.6 us (100%)
    pallas_call x1, Pallas kernels, shards(): pl.pallas_call(route_kernel, out_shape=(jax.ShapeDtypeStruct(stored_tiles...  65.3 us

profile of v4, /device:TPU:1, one launch (start us, length us, event | category | flops | bytes accessed | tf_op | source)
XLA Modules:
  0.0 66.8 jit_solution(5460308469127499214)
XLA Ops:
  0.0 65.3 %shard_map.28 = (f32[1,10,64,512]{3,2,1,0:T(8,128)S(1)}, f32[8,128]{1,0:T(8,128)S(1)}, bf16[4,2,4,64,128]{4,3,2,1,0:T(8,128)(2,1)S(1)}, bf16[8,4,4,64,128]{4,3,2...) custom-call(s32[64]{0:T(128)} %owner_any.1, f32[1,10,64,512]{3,2,1,0:T(8,128)} %tiles_ref.3), custom_call_target="tpu_custom_call" | custom-call | tf_op jit(solution)/shard_map/pallas_call | solution.py:538
  65.3 1.3 %shard_map.29 = f32[1,10,64,512]{3,2,1,0:T(8,128)} custom-call(f32[8,128]{1,0:T(8,128)S(1)} %get-tuple-element.10.size_ref, s32[64]{0:T(128)} %owner_any.1, f32[1,10,64,512]{3,2,1,0:T(8,128)} %tiles_ref.3, f32[1,10,64,512]{3,2,1,0:T(8,128)S(1)} %get-tuple-element.11.upd, bf16[4,2,4,64,128]{4,3,2,1,0:T(8,128)(2,1)S(1)} %get-tuple-element.12.fin_any, ...), custom_call_target="tpu_custom_call" | custom-call | tf_op jit(solution)/shard_map/pallas_call | solution.py:586
